TPU v7x, 512 devices: a whole 4x8x8 slice. The times are simulated.
512 devices in a mesh: section: 4 (over x), seq: 128 (over z, y, core).
Axes of the slice: x: 4, y: 8, z: 8, core: 2. Of those that a mesh axis runs over, the one named last changes fastest.
Arguments:
- hidden: bfloat16 [65536, 4096], P('seq', 'section'), may hold values from -6 to 6
- norm_gain: bfloat16 [4096], P('section'), may hold values from 0.25 to 1.75
- query_weight: bfloat16 [4096, 512], P(None, 'section')
- key_weight: bfloat16 [4096, 128], P('section')
- value_weight: bfloat16 [4096, 128], P('section'), may hold values from -0.5 to 0.5
- output_weight: bfloat16 [512, 4096], P(None, 'section'), may hold values from -0.25 to 0.25
- block_reach: int32 [512], P('seq'), may hold values from 0 to 2
- header_ids: int32 [2], replicated, may hold values from 0 to 511, as said below
Outputs:
- attention_out: bfloat16 [65536, 4096], P('seq', 'section')
Inputs may be any that keep to these rules, and one draw needn't show every extreme that they name: `header_ids`: the 2 indices are distinct block indices, and the last block, 511, is always one of them, at any position.
All inputs are finite; a program needn't handle non-finite values.
Results may differ from a plain program's by a relative error of at most 0.014.
Values may be sent and summed in bfloat16 or wider, within the bound.
No kernel may reach another device: no remote copies, remote signals or barrier semaphores. Data moves between devices by JAX's collectives and lax.ppermute only.
A program may use at most 64 MiB of HBM per device.

v0:
```python
import math
import jax
import jax.numpy as jnp
from jax import lax
from jax.sharding import PartitionSpec as P

BLOCK = 128
REACH = 2
EPSILON = 1e-05
THETA = 500000.0


def merged(value, axis, combine):
    everything = jax.tree.map(lambda part: lax.all_gather(part, axis), value)
    leading = jax.tree.map(lambda part: part[0], everything)

    def lap(k, so_far):
        return combine(so_far, jax.tree.map(lambda part: part[k], everything))

    return lax.fori_loop(1, lax.axis_size(axis), lap, leading)


def padded(cells, sides, width):
    for axis, dim in sides:
        count = lax.axis_size(axis)
        ends = count - 1
        head = lax.slice_in_dim(cells, 0, width, axis=dim)
        tail = lax.slice_in_dim(cells, cells.shape[dim] - width, cells.shape[dim], axis=dim)
        cells = jnp.concatenate(
            [
                lax.ppermute(tail, axis, [(i, (i + 1) % count) for i in range(ends)]),
                cells,
                lax.ppermute(head, axis, [((i + 1) % count, i) for i in range(ends)]),
            ],
            axis=dim,
        )
    return cells


def tables(positions, head_width):
    middle = head_width // 2
    frequency = jnp.exp(
        -(2.0 / head_width) * math.log(THETA) * jnp.arange(middle, dtype=jnp.float32)
    )
    angles = positions.astype(jnp.float32)[:, None] * frequency[None, :]
    angles = jnp.concatenate([angles, angles], axis=1)
    return (jnp.cos(angles), jnp.sin(angles))


def rotate(values, cosine_table, sine_table):
    middle = values.shape[-1] // 2
    turned = jnp.concatenate([-values[..., middle:], values[..., :middle]], axis=-1)
    return values * cosine_table + turned * sine_table


def combine_parts(earlier, later):
    first_max, first_total, first_out = earlier
    second_max, second_total, second_out = later
    overall = jnp.maximum(first_max, second_max)
    first_factor = jnp.exp(first_max - overall)
    second_factor = jnp.exp(second_max - overall)
    return (
        overall,
        first_total * first_factor + second_total * second_factor,
        first_out * first_factor[:, None] + second_out * second_factor[:, None],
    )


def on_device(
    hidden,
    norm_gain,
    query_weight,
    key_weight,
    value_weight,
    output_weight,
    block_reach,
    header_ids,
):
    row_count = hidden.shape[0]
    part_width = hidden.shape[1]
    head_width = key_weight.shape[1]
    local_blocks = row_count // BLOCK
    total_blocks = local_blocks * lax.axis_size("seq")
    seq_place = lax.axis_index("seq")
    floats = hidden.astype(jnp.float32)
    squares = lax.psum(jnp.sum(floats * floats, axis=1), "section")
    scaling = lax.rsqrt(squares / (part_width * lax.axis_size("section")) + EPSILON)
    normed_part = (floats * scaling[:, None] * norm_gain.astype(jnp.float32)[None, :]).astype(
        jnp.bfloat16
    )
    weight_rows = query_weight
    query_sum = jnp.dot(
        lax.all_gather(normed_part, "section", axis=1, tiled=True),
        weight_rows,
        preferred_element_type=jnp.float32,
    )
    key_sum, value_sum = lax.psum(
        (
            jnp.dot(normed_part, key_weight, preferred_element_type=jnp.float32),
            jnp.dot(normed_part, value_weight, preferred_element_type=jnp.float32),
        ),
        "section",
    )
    positions = seq_place * row_count + jnp.arange(row_count, dtype=jnp.int32)
    cosine_table, sine_table = tables(positions, head_width)
    queries = rotate(query_sum, cosine_table, sine_table).astype(jnp.bfloat16)
    keys_here = rotate(key_sum, cosine_table, sine_table).astype(jnp.bfloat16)
    values_here = value_sum.astype(jnp.bfloat16)
    packed = jnp.concatenate([queries, keys_here, values_here], axis=1)
    block_numbers = seq_place * local_blocks + jnp.arange(local_blocks, dtype=jnp.int32)
    select = header_ids[:, None] == block_numbers[None, :]
    shaped = packed.reshape(local_blocks, BLOCK, 3 * head_width)
    picked = jnp.einsum(
        "hb,bre->hre", select.astype(jnp.bfloat16), shaped, preferred_element_type=jnp.float32
    )
    header_pack = lax.psum(picked, "seq").astype(jnp.bfloat16).reshape(-1, 3 * head_width)
    head_queries = header_pack[:, :head_width]
    head_keys = header_pack[:, head_width : 2 * head_width]
    head_values = header_pack[:, 2 * head_width :]
    inverse_root = 1.0 / math.sqrt(head_width)
    far_scores = (
        jnp.einsum("qd,kd->qk", head_queries, keys_here, preferred_element_type=jnp.float32)
        * inverse_root
    )
    far_max = jnp.max(far_scores, axis=1)
    far_weights = jnp.exp(far_scores - far_max[:, None])
    far_total = jnp.sum(far_weights, axis=1)
    far_out = jnp.dot(
        far_weights.astype(jnp.bfloat16), values_here, preferred_element_type=jnp.float32
    )
    merged_max, merged_total, merged_out = merged(
        (far_max, far_total, far_out), "seq", combine_parts
    )
    header_result = merged_out / merged_total[:, None]
    margin_rows = REACH * BLOCK
    stacked = jnp.concatenate([keys_here, values_here], axis=1)
    extended = padded(stacked, (("seq", 0),), margin_rows)
    near_keys = extended[:, :head_width]
    near_values = extended[:, head_width:]
    extent = row_count + 2 * margin_rows
    key_blocks = seq_place * local_blocks - REACH + jnp.arange(extent, dtype=jnp.int32) // BLOCK
    query_blocks = seq_place * local_blocks + jnp.arange(row_count, dtype=jnp.int32) // BLOCK
    limits = jnp.repeat(block_reach, BLOCK)
    key_header = jnp.any(header_ids[:, None] == key_blocks[None, :], axis=0)
    allowed = (key_blocks >= 0)[None, :] & (key_blocks < total_blocks)[None, :]
    allowed = allowed & (jnp.abs(key_blocks[None, :] - query_blocks[:, None]) <= limits[:, None])
    allowed = allowed & jnp.logical_not(key_header)[None, :]
    near_scores = (
        jnp.einsum("qd,kd->qk", queries, near_keys, preferred_element_type=jnp.float32)
        * inverse_root
    )
    near_scores = jnp.where(allowed, near_scores, -jnp.inf)
    head_scores = (
        jnp.einsum("qd,kd->qk", queries, head_keys, preferred_element_type=jnp.float32)
        * inverse_root
    )
    scores = jnp.concatenate([near_scores, head_scores], axis=1)
    row_top = jnp.max(scores, axis=1)
    weights = jnp.exp(scores - row_top[:, None])
    row_sums = jnp.sum(weights, axis=1)
    joined = jnp.concatenate([near_values, head_values], axis=0)
    mixed_out = (
        jnp.dot(weights.astype(jnp.bfloat16), joined, preferred_element_type=jnp.float32)
        / row_sums[:, None]
    )
    header_local = jnp.einsum(
        "hb,hre->bre", select.astype(jnp.float32), header_result.reshape(-1, BLOCK, head_width)
    )
    is_local_header = jnp.any(select, axis=0)
    attended = jnp.where(
        is_local_header[:, None, None],
        header_local,
        mixed_out.reshape(local_blocks, BLOCK, head_width),
    )
    attended = attended.reshape(row_count, head_width).astype(jnp.bfloat16)
    weight_rows = output_weight
    result = jnp.dot(
        lax.all_gather(attended, "section", axis=1, tiled=True),
        weight_rows,
        preferred_element_type=jnp.float32,
    )
    return result.astype(jnp.bfloat16)


def solution(mesh):
    return jax.shard_map(
        on_device,
        mesh=mesh,
        in_specs=(
            P("seq", "section"),
            P("section"),
            P(None, "section"),
            P("section", None),
            P("section", None),
            P(None, "section"),
            P("seq"),
            P(),
        ),
        out_specs=P("seq", "section"),
        check_vma=False,
    )
```

profile of v0, /device:TPU:64, one launch (start us, length us, event | category | flops | bytes accessed | tf_op | source)
XLA Modules:
  0.0 913.6 jit_solution(16988144689448362159)
XLA Ops:
  7.3 1.5 fusion.2
  8.8 10.5 %psum.28 = f32[512]{0:T(512)S(1)} all-reduce(f32[512]{0:T(512)S(1)} %fusion.2), channel_id=1, replica_groups=mesh['section'=4,'seq'=128] {'section'}, use_global_device_ids=true, to_apply=%region_2.0 | all-reduce | flops 512 | bytes 4096 | tf_op jit(solution)/shard_map/psum | solution.py:86
  19.3 1.6 fusion.4
  20.9 1.2 fusion.53
  23.0 1.7 fusion.54
  24.8 17.2 %all-reduce.5 = bf16[512,128]{0,1:T(8,128)(2,1)S(1)} all-reduce(f32[512,128]{0,1:T(8,128)S(1)} %fusion.54), channel_id=1, replica_groups=mesh['section'=4,'seq'=128] {'section'}, use_global_device_ids=true, to_apply=%region_4.0 | all-reduce | flops 65536 | bytes 393216 | tf_op jit(solution)/shard_map/psum | solution.py:97
  42.0 34.5 %all-reduce.4.cloned.1.call-done = f32[512,128]{0,1:T(8,128)} async-done(((f32[512,128]{0,1:T(8,128)}), f32[512,128]{0,1:T(8,128)}) %all-reduce.4.cloned.1.call-update) | async-done | bytes 262160 | tf_op jit(solution)/shard_map/psum | solution.py:97
  77.5 55.5 %all-gather.8.cloned.1.call-done = bf16[512,4096]{1,0:T(8,128)(2,1)} async-done(((bf16[512,1024]{1,0:T(8,128)(2,1)}), bf16[512,4096]{1,0:T(8,128)(2,1)}) %all-gather.8.cloned.1.call-update) | async-done | bytes 4194320 | tf_op jit(solution)/shard_map/all_gather | solution.py:93
  133.0 3.7 fusion.52
  138.7 461.0 %all-reduce.6 = bf16[2,128,384]{2,0,1:T(2,128)(2,1)S(1)} all-reduce(f32[2,128,384]{2,0,1:T(2,128)S(1)} %fusion.48), channel_id=1, replica_groups=mesh['section'=4,'seq'=128] {'seq'}, use_global_device_ids=true, to_apply=%region_5.0 | all-reduce | flops 98304 | bytes 589824 | tf_op jit(solution)/shard_map/psum | solution.py:116
  601.6 82.4 %all-gather.3 = f32[128,1,256]{2,1,0:T(1,128)S(1)} all-gather(f32[1,1,256]{2,1,0:T(1,128)S(1)} %bitcast.66), channel_id=2, replica_groups=mesh['section'=4,'seq'=128] {'seq'}, dimensions={0}, use_global_device_ids=true | all-gather | bytes 132096 | tf_op jit(solution)/shard_map/all_gather | solution.py:14
  684.3 47.1 %all-gather.4 = f32[128,1,256]{2,1,0:T(1,128)S(1)} all-gather(f32[1,1,256]{2,1,0:T(1,128)S(1)} %bitcast.67), channel_id=3, replica_groups=mesh['section'=4,'seq'=128] {'seq'}, dimensions={0}, use_global_device_ids=true | all-gather | bytes 132096 | tf_op jit(solution)/shard_map/all_gather | solution.py:14
  731.4 4.6 collective-permute-start.1
  736.0 1.9 collective-permute-start
  738.5 5.9 collective-permute-done
  748.1 144.2 %while.19 = (s32[]{:T(128)}, f32[256]{0:T(256)S(1)}, f32[256]{0:T(256)S(1)}, f32[256,128]{1,0:T(8,128)S(1)}, f32[128,256]{1,0:T(8,128)S(1)}, /*index=5*/f32[128,...) while((s32[]{:T(128)}, f32[256]{0:T(256)S(1)}, f32[256]{0:T(256)S(1)}, ...), condition=%wide.region_9.10_spmd, body=%wide.region_8.0_spmd.sunk | while | flops 99845 | bytes 407703 | solution.py:20
  749.3 1.1 fusion.69
  751.5 1.1 fusion.69
  753.8 1.1 fusion.69
  754.9 1.1 fusion.69
  756.1 1.1 fusion.69
  757.2 1.1 fusion.69
  758.3 1.1 fusion.69
  759.5 1.1 fusion.69
  761.7 1.1 fusion.69
  764.0 1.1 fusion.69
  766.3 1.1 fusion.69
  768.6 1.1 fusion.69
  770.8 1.1 fusion.69
  773.1 1.1 fusion.69
  892.8 12.6 %all_gather.31 = bf16[512,512]{1,0:T(8,128)(2,1)S(1)} all-gather(bf16[512,128]{1,0:T(8,128)(2,1)S(1)} %bitcast.59), channel_id=1, replica_groups=mesh['section'=4,'seq'=128] {'section'}, dimensions={1}, use_global_device_ids=true | all-gather | bytes 655360 | tf_op jit(solution)/shard_map/all_gather | solution.py:178
  905.4 1.7 convolution_convert_fusion
  (442 shorter events, 136.4 us)
Async XLA Ops:
  6.5 898.9 %copy-start = (bf16[512,1024]{1,0:T(8,128)(2,1)S(1)}, bf16[512,1024]{1,0:T(8,128)(2,1)}, u32[]{:S(2)}) copy-start(bf16[512,1024]{1,0:T(8,128)(2,1)} %param.15) | copy-start | bytes 3145732
  6.5 14.4 %copy-start.7 = (bf16[1024,128]{1,0:T(8,128)(2,1)S(1)}, bf16[1024,128]{1,0:T(8,128)(2,1)}, u32[]{:S(2)}) copy-start(bf16[1024,128]{1,0:T(8,128)(2,1)} %param.13) | copy-start | bytes 786436
  6.5 70.0 %all-reduce.4.cloned.1.call-start = ((), (), s32[]{:S(2)}) async-start(), calls=%async_computation.1 | async-start | bytes 524288 | tf_op jit(solution)/shard_map/psum | solution.py:97
  19.3 3.6 copy-start.8
  20.9 1.3 copy-start.1
  22.1 110.9 %copy-start.4 = (bf16[4096,128]{1,0:T(8,128)(2,1)S(1)}, bf16[4096,128]{1,0:T(8,128)(2,1)}, u32[]{:S(2)}) copy-start(bf16[4096,128]{1,0:T(8,128)(2,1)} %param.12) | copy-start | bytes 3145732
  22.2 110.8 %all-gather.8.cloned.1.call-start = ((), (), s32[]{:S(2)}) async-start(), calls=%async_computation | async-start | bytes 5242880 | tf_op jit(solution)/shard_map/all_gather | solution.py:93
  22.9 724.2 %all-gather.10.cloned.1.call-start = ((), (), s32[]{:S(2)}) async-start(), calls=%async_computation.2 | async-start | bytes 16908288 | tf_op jit(solution)/shard_map/all_gather | solution.py:14
  77.5 59.2 %copy-start.3 = (f32[512,128]{0,1:T(8,128)S(1)}, f32[512,128]{0,1:T(8,128)}, u32[]{:S(2)}) copy-start(f32[512,128]{0,1:T(8,128)} %all-reduce.4.cloned.1.call-done) | copy-start | bytes 786436
  136.7 1.6 copy-start.9
  138.3 463.3 %copy-start.10 = (s32[4]{0:T(128)S(1)}, s32[4]{0:T(128)}, u32[]{:S(2)}) copy-start(s32[4]{0:T(128)} %param.16) | copy-start | bytes 52
  684.1 61.5 %copy-start.6 = (f32[128,1,256]{2,1,0:T(1,128)}, f32[128,1,256]{2,1,0:T(1,128)S(1)}, u32[]{:S(2)}) copy-start(f32[128,1,256]{2,1,0:T(1,128)S(1)} %all-gather.3) | copy-start | bytes 393220
  731.4 14.1 %copy-start.5 = (f32[128,1,256]{2,1,0:T(1,128)}, f32[128,1,256]{2,1,0:T(1,128)S(1)}, u32[]{:S(2)}) copy-start(f32[128,1,256]{2,1,0:T(1,128)S(1)} %all-gather.4) | copy-start | bytes 393220
  731.4 7.1 collective-permute-start.1
  736.0 8.4 collective-permute-start
  744.5 1.1 copy-start.2
  745.6 1.0 slice-start
  746.5 1.5 slice-start.1
  746.5 1.5 slice-start.2
Sparse Core Ops, SparseCore 0:
  22.3 54.2 all-reduce.3
  78.9 54.1 all-gather.7
  601.4 126.7 all-gather.9
where the time goes:
time: 916 us; the launch traced here: 914 us
  blocking collectives  631 us (69%)
  other arithmetic  146 us (16%)
  waiting for transfers between devices  96.8 us (11%)
  between operations  13.5 us (1%)
  matrix products  12.3 us (1%)
    psum x1, blocking collectives, on_device(): lax.psum(picked, 'seq').astype(jnp.bfloat16).reshape(-1, 3 * head_width)  461 us
    add x127, other arithmetic, combine_parts(): first_out * first_factor[:, None] + second_out * second_factor[:, None]  136 us
    all_gather x2, blocking collectives, merged(): everything = jax.tree.map(lambda part: lax.all_gather(part, axis), value)  130 us
    all_gather x1, waiting for transfers between devices, on_device(): lax.all_gather(normed_part, 'section', axis=1, tiled=True)  55.5 us
    psum x1, waiting for transfers between devices, on_device(): lax.psum((jnp.dot(normed_part, key_weight, preferred_element_type=jnp.flo...  34.5 us
  transfers between devices with their start and end apart: 5, of which 4 were waited for; matrix products, arithmetic and copies ran while one was open for 1% of the time, Pallas kernels for 0%

commit v1 on v0

--- a/solution.py
+++ b/solution.py
@@ -8,6 +8,22 @@
 REACH = 2
 EPSILON = 1e-05
 THETA = 500000.0
+
+
+def collect(x, axis, dim):
+    ways, here, step = (lax.axis_size(axis), lax.axis_index(axis), x.shape[dim])
+    dims = [n * ways if d == dim else n for d, n in enumerate(x.shape)]
+    full = lax.dynamic_update_slice_in_dim(jnp.zeros(dims, x.dtype), x, here * step, axis=dim)
+    going_up = going_down = x
+    for far in range(1, ways // 2 + 1):
+        going_up = lax.ppermute(going_up, axis, [(d, (d + 1) % ways) for d in range(ways)])
+        full = lax.dynamic_update_slice_in_dim(full, going_up, (here - far) % ways * step, axis=dim)
+        if 2 * far < ways:
+            going_down = lax.ppermute(going_down, axis, [(d, (d - 1) % ways) for d in range(ways)])
+            full = lax.dynamic_update_slice_in_dim(
+                full, going_down, (here + far) % ways * step, axis=dim
+            )
+    return full
 
 
 def merged(value, axis, combine):
@@ -90,9 +106,7 @@
     )
     weight_rows = query_weight
     query_sum = jnp.dot(
-        lax.all_gather(normed_part, "section", axis=1, tiled=True),
-        weight_rows,
-        preferred_element_type=jnp.float32,
+        collect(normed_part, "section", 1), weight_rows, preferred_element_type=jnp.float32
     )
     key_sum, value_sum = lax.psum(
         (

time: 916 us -> 881 us (0.962)
  waiting for transfers between devices: 96.8 us -> 22.4 us
  blocking collectives: 631 us -> 652 us
    all_gather x1 -> x0, waiting for transfers between devices: 55.5 us -> none  [on_device(): lax.all_gather(normed_part, 'section', axis=1, tiled=True)]
    psum x1, waiting for transfers between devices: 34.5 us -> 0.02 us  [on_device(): lax.psum((jnp.dot(normed_part, key_weight, preferred_element_type=jnp.flo...]
    psum x1, blocking collectives: 17.2 us -> 36.8 us  [on_device(): lax.psum((jnp.dot(normed_part, key_weight, preferred_element_type=jnp.flo...]
    ppermute x0 -> x3, waiting for transfers between devices: none -> 16.2 us  [the longest x2 16.2 us: collect(): lax.ppermute(going_up, axis, [(d, (d + 1) % ways) for d in range(ways)])]
  transfers between devices with their start and end apart: 5 -> 7, of which waited for: 4 -> 3; matrix products, arithmetic and copies ran while one was open for 1% -> 1% of each run, Pallas kernels for 0% -> 0%
where the time goes in v1:
time: 881 us; the launch traced here: 878 us
  blocking collectives  652 us (74%)
  other arithmetic  146 us (17%)
  waiting for transfers between devices  22.4 us (3%)
  starting transfers between devices  15.5 us (2%)
  between operations  13.8 us (2%)
  matrix products  12.1 us (1%)
  local copies, waits for them, and re-layouts  11.9 us (1%)
    psum x1, blocking collectives, on_device(): lax.psum(picked, 'seq').astype(jnp.bfloat16).reshape(-1, 3 * head_width)  463 us
    add x127, other arithmetic, combine_parts(): first_out * first_factor[:, None] + second_out * second_factor[:, None]  136 us
    all_gather x2, blocking collectives, merged(): everything = jax.tree.map(lambda part: lax.all_gather(part, axis), value)  130 us
    psum x1, blocking collectives, on_device(): lax.psum((jnp.dot(normed_part, key_weight, preferred_element_type=jnp.flo...  36.8 us
  transfers between devices with their start and end apart: 7, of which 3 were waited for; matrix products, arithmetic and copies ran while one was open for 1% of the time, Pallas kernels for 0%

profile of v1, /device:TPU:64, one launch (start us, length us, event | category | flops | bytes accessed | tf_op | source)
XLA Modules:
  0.0 878.4 jit_solution(1184531812036470500)
XLA Ops:
  7.3 1.6 fusion.2
  8.9 10.5 %psum.28 = f32[512]{0:T(512)S(1)} all-reduce(f32[512]{0:T(512)S(1)} %fusion.2), channel_id=1, replica_groups=mesh['section'=4,'seq'=128] {'section'}, use_global_device_ids=true, to_apply=%region_2.3 | all-reduce | flops 512 | bytes 4096 | tf_op jit(solution)/shard_map/psum | solution.py:102
  19.4 2.5 broadcast_in_dim.19
  21.9 1.3 constant_dynamic-update-slice_fusion.3
  23.2 1.9 collective-permute-start
  25.1 5.1 collective-permute-start.1
  30.3 1.2 fusion.54
  31.6 1.4 fusion.55
  33.0 16.2 %collective-permute-done = bf16[512,1024]{1,0:T(8,128)(2,1)S(1)} collective-permute-done((bf16[512,1024]{1,0:T(8,128)(2,1)S(1)}, bf16[512,1024]{1,0:T(8,128)(2,1)S(1)}, u32[]{:S(2)}, u32[]{:S(2)}) %collective-permute-start) | collective-permute-done | bytes 1048608 | tf_op jit(solution)/shard_map/ppermute | solution.py:19
  49.2 1.9 collective-permute-start.2
  51.9 36.8 %all-reduce.5 = bf16[512,128]{0,1:T(8,128)(2,1)S(1)} all-reduce(f32[512,128]{0,1:T(8,128)S(1)} %fusion.55), channel_id=1, replica_groups=mesh['section'=4,'seq'=128] {'section'}, use_global_device_ids=true, to_apply=%region_4.5 | all-reduce | flops 65536 | bytes 393216 | tf_op jit(solution)/shard_map/psum | solution.py:111
  90.8 2.5 constant_dynamic-update-slice_fusion.1
  93.3 2.3 constant_dynamic-update-slice_fusion
  95.6 3.7 fusion.53
  101.3 462.8 %all-reduce.6 = bf16[2,128,384]{2,0,1:T(2,128)(2,1)S(1)} all-reduce(f32[2,128,384]{2,0,1:T(2,128)S(1)} %fusion.48), channel_id=1, replica_groups=mesh['section'=4,'seq'=128] {'seq'}, use_global_device_ids=true, to_apply=%region_5.6 | all-reduce | flops 98304 | bytes 589824 | tf_op jit(solution)/shard_map/psum | solution.py:130
  566.1 82.4 %all-gather.3 = f32[128,1,256]{2,1,0:T(1,128)S(1)} all-gather(f32[1,1,256]{2,1,0:T(1,128)S(1)} %bitcast.66), channel_id=2, replica_groups=mesh['section'=4,'seq'=128] {'seq'}, dimensions={0}, use_global_device_ids=true | all-gather | bytes 132096 | tf_op jit(solution)/shard_map/all_gather | solution.py:30
  648.7 47.1 %all-gather.4 = f32[128,1,256]{2,1,0:T(1,128)S(1)} all-gather(f32[1,1,256]{2,1,0:T(1,128)S(1)} %bitcast.67), channel_id=3, replica_groups=mesh['section'=4,'seq'=128] {'seq'}, dimensions={0}, use_global_device_ids=true | all-gather | bytes 132096 | tf_op jit(solution)/shard_map/all_gather | solution.py:30
  695.9 4.5 collective-permute-start.4
  700.4 1.9 collective-permute-start.3
  702.9 5.9 collective-permute-done.3
  712.5 144.2 %while.19 = (s32[]{:T(128)}, f32[256]{0:T(256)S(1)}, f32[256]{0:T(256)S(1)}, f32[256,128]{1,0:T(8,128)S(1)}, f32[128,256]{1,0:T(8,128)S(1)}, /*index=5*/f32[128,...) while((s32[]{:T(128)}, f32[256]{0:T(256)S(1)}, f32[256]{0:T(256)S(1)}, ...), condition=%wide.region_9.10_spmd, body=%wide.region_8.9_spmd.sunk | while | flops 99845 | bytes 407703 | solution.py:36
  713.7 1.1 fusion.70
  715.9 1.1 fusion.70
  718.2 1.1 fusion.70
  720.5 1.1 fusion.70
  722.7 1.1 fusion.70
  723.9 1.1 fusion.70
  725.0 1.1 fusion.70
  726.2 1.1 fusion.70
  727.3 1.1 fusion.70
  857.2 12.6 %all_gather.27 = bf16[512,512]{1,0:T(8,128)(2,1)S(1)} all-gather(bf16[512,128]{1,0:T(8,128)(2,1)S(1)} %bitcast.59), channel_id=1, replica_groups=mesh['section'=4,'seq'=128] {'section'}, dimensions={1}, use_global_device_ids=true | all-gather | bytes 655360 | tf_op jit(solution)/shard_map/all_gather | solution.py:192
  869.8 1.7 convolution_convert_fusion
  (449 shorter events, 142.8 us)
Async XLA Ops:
  6.5 863.3 %copy-start = (bf16[512,1024]{1,0:T(8,128)(2,1)S(1)}, bf16[512,1024]{1,0:T(8,128)(2,1)}, u32[]{:S(2)}) copy-start(bf16[512,1024]{1,0:T(8,128)(2,1)} %param.15) | copy-start | bytes 3145732
  6.5 82.2 %all-reduce.4.cloned.1.call-start = ((), (), s32[]{:S(2)}) async-start(), calls=%async_computation | async-start | bytes 524288 | tf_op jit(solution)/shard_map/psum | solution.py:111
  7.3 14.6 %copy-start.1 = (bf16[512,1024]{1,0:T(8,128)(2,1)S(1)}, bf16[512,1024]{1,0:T(8,128)(2,1)}, u32[]{:S(2)}) copy-start(bf16[512,1024]{1,0:T(8,128)(2,1)} %param.10) | copy-start | bytes 3145732
  21.9 8.4 copy-start.8
  23.2 26.0 %collective-permute-start = (bf16[512,1024]{1,0:T(8,128)(2,1)S(1)}, bf16[512,1024]{1,0:T(8,128)(2,1)S(1)}, u32[]{:S(2)}, u32[]{:S(2)}) collective-permute-start(bf16[512,1024]{1,0:T(8,128)(2,1)S(1)} %get-tuple-element.203), channel_id=1, source_target_pairs={{0,128},{128,256},{256,384},{384,0},{1,129},{129,257},{257,385},{3... | collective-permute-start | bytes 3145736 | tf_op jit(solution)/shard_map/ppermute | solution.py:19
  25.1 65.7 %collective-permute-start.1 = (bf16[512,1024]{1,0:T(8,128)(2,1)S(1)}, bf16[512,1024]{1,0:T(8,128)(2,1)}, u32[]{:S(2)}, u32[]{:S(2)}) collective-permute-start(bf16[512,1024]{1,0:T(8,128)(2,1)S(1)} %get-tuple-element.203), channel_id=1, source_target_pairs={{0,384},{128,0},{256,128},{384,256},{1,385},{129,1},{257,129},{385... | collective-permute-start | bytes 3145736 | tf_op jit(solution)/shard_map/ppermute | solution.py:22
  31.5 680.0 %all-gather.7.cloned.1.call-start = ((), (), s32[]{:S(2)}) async-start(), calls=%async_computation.1 | async-start | bytes 16908288 | tf_op jit(solution)/shard_map/all_gather | solution.py:30
  49.2 44.1 %collective-permute-start.2 = (bf16[512,1024]{1,0:T(8,128)(2,1)S(1)}, bf16[512,1024]{1,0:T(8,128)(2,1)}, u32[]{:S(2)}, u32[]{:S(2)}) collective-permute-start(bf16[512,1024]{1,0:T(8,128)(2,1)S(1)} %collective-permute-done), channel_id=1, source_target_pairs={{0,128},{128,256},{256,384},{384,0},{1,129},{129,257},{257,385},{3... | collective-permute-start | bytes 3145736 | tf_op jit(solution)/shard_map/ppermute | solution.py:19
  90.8 4.8 copy-start.4
  95.6 3.8 copy-start.3
  95.6 3.8 copy-start.7
  99.3 1.6 copy-start.9
  100.5 465.5 %copy-start.10 = (s32[4]{0:T(128)S(1)}, s32[4]{0:T(128)}, u32[]{:S(2)}) copy-start(s32[4]{0:T(128)} %param.16) | copy-start | bytes 52
  648.5 61.5 %copy-start.6 = (f32[128,1,256]{2,1,0:T(1,128)}, f32[128,1,256]{2,1,0:T(1,128)S(1)}, u32[]{:S(2)}) copy-start(f32[128,1,256]{2,1,0:T(1,128)S(1)} %all-gather.3) | copy-start | bytes 393220
  695.8 14.1 %copy-start.5 = (f32[128,1,256]{2,1,0:T(1,128)}, f32[128,1,256]{2,1,0:T(1,128)S(1)}, u32[]{:S(2)}) copy-start(f32[128,1,256]{2,1,0:T(1,128)S(1)} %all-gather.4) | copy-start | bytes 393220
  695.9 7.1 collective-permute-start.4
  700.4 8.4 collective-permute-start.3
  708.9 1.1 copy-start.2
  710.0 1.0 slice-start
  710.9 1.5 slice-start.1
  710.9 1.5 slice-start.2
Sparse Core Ops, SparseCore 0:
  31.6 54.1 all-reduce.3
  565.9 125.5 all-gather.6
